TPU v7x, 256 devices: a whole 4x4x8 slice. The times are simulated.
256 devices in a mesh: seq: 32 (over y, z), mp: 8 (over x, core).
Axes of the slice: x: 4, y: 4, z: 8, core: 2. Of those that a mesh axis runs over, the one named last changes fastest.
Arguments:
- queries: bfloat16 [512, 8192], P('seq', 'mp'), may hold values from -64 to 64
- prefix_keys: bfloat16 [131072, 1024], P('seq', 'mp'), may hold values from -24 to 24
- prefix_values: bfloat16 [131072, 1024], P('seq', 'mp'), may hold values from -6 to 6
- resp_keys: bfloat16 [512, 1024], P('seq', 'mp'), may hold values from -28 to 28
- resp_values: bfloat16 [512, 1024], P('seq', 'mp'), may hold values from -6 to 6
- segment_ids: int32 [512], replicated, may hold values from 0 to 3, never falling along the last dimension, each value on 1 to 256 neighbouring positions
- out_weight: bfloat16 [8192, 8192], P('mp', 'seq'), may hold values from -0.0625 to 0.0625
Outputs:
- scored: bfloat16 [512, 8192], P('mp', 'seq')
Inputs may be any that keep to these rules, and one draw needn't show every extreme that they name: `segment_ids`: never falling; each of the 4 responses holds 1 to 256 tokens, one exactly 256.
All inputs are finite; a program needn't handle non-finite values.
Results may differ from a plain program's by a relative error of at most 0.013.
Values may be sent and summed in bfloat16 or wider, within the bound.
No kernel may reach another device: no remote copies, remote signals or barrier semaphores. Data moves between devices by JAX's collectives and lax.ppermute only.
A program may use at most 64 MiB of HBM per device.

v0:
```python
import jax
import jax.numpy as jnp
from jax import lax
from jax.sharding import PartitionSpec as P

HD = 128


def update(state, scores, value_block):
    peak, total, weighted = state
    new_peak = jnp.maximum(peak, jnp.max(scores, axis=2))
    factor = jnp.exp(peak - new_peak)
    weights = jnp.exp(scores - new_peak[..., None])
    total = total * factor + jnp.sum(weights, axis=2)
    product = jnp.einsum(
        "kmn,nkd->kmd",
        weights.astype(jnp.bfloat16),
        value_block,
        preferred_element_type=jnp.float32,
    )
    return (new_peak, total, weighted * factor[..., None] + product)


def on_device(queries, prefix_keys, prefix_values, resp_keys, resp_values, segment_ids, out_weight):
    all_queries, all_keys, all_values = (
        lax.all_gather(queries, "seq", axis=0, tiled=True),
        lax.all_gather(resp_keys, "seq", axis=0, tiled=True),
        lax.all_gather(resp_values, "seq", axis=0, tiled=True),
    )
    resp_rows = all_queries.shape[0]
    kv_local = resp_keys.shape[1] // HD
    group = all_queries.shape[1] // (kv_local * HD)
    width = resp_rows * group
    scale = HD ** (-0.5)
    query_heads = (
        all_queries.reshape(resp_rows, kv_local, group, HD)
        .transpose(1, 0, 2, 3)
        .reshape(kv_local, width, HD)
    )
    plen = prefix_keys.shape[0]
    block = min(512, plen)
    keys_local = prefix_keys.reshape(plen, kv_local, HD)
    values_local = prefix_values.reshape(plen, kv_local, HD)
    own_keys = all_keys.reshape(resp_rows, kv_local, HD)
    own_values = all_values.reshape(resp_rows, kv_local, HD)

    def prefix_step(index, state):
        start = index * block
        key_block = lax.dynamic_slice_in_dim(keys_local, start, block, 0)
        value_block = lax.dynamic_slice_in_dim(values_local, start, block, 0)
        scores = (
            jnp.einsum("kmd,nkd->kmn", query_heads, key_block, preferred_element_type=jnp.float32)
            * scale
        )
        return update(state, scores, value_block)

    start_state = (
        jnp.full((kv_local, width), -1e30, jnp.float32),
        jnp.zeros((kv_local, width), jnp.float32),
        jnp.zeros((kv_local, width, HD), jnp.float32),
    )
    state = lax.fori_loop(0, plen // block, prefix_step, start_state)
    top = lax.pmax(state[0], "seq")
    factor = jnp.exp(state[0] - top)
    total, weighted = lax.psum((state[1] * factor, state[2] * factor[..., None]), "seq")
    scores = (
        jnp.einsum("kmd,nkd->kmn", query_heads, own_keys, preferred_element_type=jnp.float32)
        * scale
    )
    row_token = jnp.arange(width, dtype=jnp.int32) // group
    columns = jnp.arange(resp_rows, dtype=jnp.int32)
    allowed = (segment_ids[row_token][:, None] == segment_ids[None, :]) & (
        columns[None, :] <= row_token[:, None]
    )
    scores = jnp.where(allowed[None], scores, jnp.float32(-1e30))
    final = update((top, total, weighted), scores, own_values)
    heads = (final[2] / final[1][..., None]).astype(jnp.bfloat16)
    attended = (
        heads.reshape(kv_local, resp_rows, group, HD)
        .transpose(1, 0, 2, 3)
        .reshape(resp_rows, kv_local * group * HD)
    )
    scored = lax.psum_scatter(
        jnp.dot(attended, out_weight, preferred_element_type=jnp.float32),
        "mp",
        scatter_dimension=0,
        tiled=True,
    )
    return scored.astype(jnp.bfloat16)


def solution(mesh):
    in_specs = (
        P("seq", "mp"),
        P("seq", "mp"),
        P("seq", "mp"),
        P("seq", "mp"),
        P("seq", "mp"),
        P(),
        P("mp", "seq"),
    )
    out_specs = P("mp", "seq")
    return jax.shard_map(
        on_device, mesh=mesh, in_specs=in_specs, out_specs=out_specs, check_vma=False
    )
```

profile of v0, /device:TPU:1, one launch (start us, length us, event | category | flops | bytes accessed | tf_op | source)
XLA Modules:
  0.0 587.1 jit_solution(5276021881986632441)
XLA Ops:
  7.4 25.8 %gather_fusion = s32[4096]{0:T(1024)S(1)} fusion(s32[512]{0:T(512)S(1)} %copy-done.1, s32[4096]{0:T(1024)S(1)} %broadcast_clamp_fusion), kind=kCustom, calls=%fused_computation | custom fusion | bytes 49152 | tf_op jit(solution)/shard_map/gather | solution.py:72
  33.3 38.9 %all_gather.10 = bf16[512,128]{1,0:T(8,128)(2,1)S(1)} all-gather(bf16[16,128]{1,0:T(8,128)(2,1)S(1)} %copy-done.3), channel_id=1, replica_groups=mesh['seq'=32,'mp'=8] {'seq'}, dimensions={0}, use_global_device_ids=true | all-gather | bytes 135168 | tf_op jit(solution)/shard_map/all_gather | solution.py:27
  72.2 13.6 %all-gather.2.cloned.1.call-done = bf16[512,1024]{1,0:T(8,128)(2,1)} async-done(((bf16[16,1024]{1,0:T(8,128)(2,1)}), bf16[512,1024]{1,0:T(8,128)(2,1)}) %all-gather.2.cloned.1.call-update) | async-done | bytes 1048592 | tf_op jit(solution)/shard_map/all_gather | solution.py:26
  85.8 2.3 reshape_transpose_reshape.6
  88.1 119.4 %while.18 = (s32[]{:T(128)}, f32[1,4096]{1,0:T(1,128)S(1)}, f32[1,4096]{1,0:T(1,128)S(1)}, f32[1,4096,128]{2,1,0:T(8,128)S(1)}, bf16[4096,1,128]{2,0,1:T(8,128)(...) while((s32[]{:T(128)}, f32[1,4096]{1,0:T(1,128)S(1)}, ...), condition=%wide.region_3.0_spmd.clone, body=%wide.region_0.0_spmd.clone.sunk | while | flops 1092112384 | bytes 64487624 | solution.py:62
  88.1 5.8 multiply_reduce_fusion.2
  93.9 4.9 fusion.46
  98.9 0.8 copy-done.2
  99.6 3.3 fusion.48
  103.0 5.8 multiply_reduce_fusion.2
  108.8 4.9 fusion.46
  113.8 0.8 copy-done.2
  114.5 3.3 fusion.48
  117.9 5.8 multiply_reduce_fusion.2
  123.7 4.9 fusion.46
  128.7 0.8 copy-done.2
  129.5 3.3 fusion.48
  132.8 5.8 multiply_reduce_fusion.2
  138.6 4.9 fusion.46
  143.6 0.8 copy-done.2
  144.4 3.3 fusion.48
  147.8 5.8 multiply_reduce_fusion.2
  153.6 4.9 fusion.46
  158.6 0.8 copy-done.2
  159.3 3.3 fusion.48
  162.7 5.8 multiply_reduce_fusion.2
  168.5 4.9 fusion.46
  174.2 3.3 fusion.48
  177.6 5.8 multiply_reduce_fusion.2
  183.4 4.9 fusion.46
  188.4 0.8 copy-done.2
  189.2 3.3 fusion.48
  192.5 5.8 multiply_reduce_fusion.2
  198.3 4.9 fusion.46
  203.3 0.8 copy-done.2
  204.1 3.3 fusion.48
  207.4 112.3 %pmax.7 = f32[1,4096]{1,0:T(1,128)S(1)} all-reduce(f32[1,4096]{1,0:T(1,128)S(1)} %get-tuple-element.132), channel_id=1, replica_groups=mesh['seq'=32,'mp'=8] {'seq'}, use_global_device_ids=true, to_apply=%region_4.0 | all-reduce | flops 4096 | bytes 32768 | tf_op jit(solution)/shard_map/pmax | solution.py:63
  319.7 2.3 reshape.129
  322.0 5.7 fusion.30
  327.8 1.9 broadcast_multiply_fusion
  329.8 30.9 %all_gather.11 = bf16[512,128]{1,0:T(8,128)(2,1)S(1)} all-gather(bf16[16,128]{1,0:T(8,128)(2,1)S(1)} %copy-done.4), channel_id=1, replica_groups=mesh['seq'=32,'mp'=8] {'seq'}, dimensions={0}, use_global_device_ids=true | all-gather | bytes 135168 | tf_op jit(solution)/shard_map/all_gather | solution.py:28
  360.7 112.4 %psum.15 = f32[1,4096]{1,0:T(1,128)S(1)} all-reduce(f32[1,4096]{1,0:T(1,128)S(1)} %get-tuple-element.176), channel_id=1, replica_groups=mesh['seq'=32,'mp'=8] {'seq'}, use_global_device_ids=true, to_apply=%region_7.8 | all-reduce | flops 4096 | bytes 32768 | tf_op jit(solution)/shard_map/psum | solution.py:65
  473.1 4.5 fusion.19
  477.7 28.6 %all-reduce.2.cloned.1.call-done = f32[1,4096,128]{2,1,0:T(8,128)} async-done(((f32[1,4096,128]{2,1,0:T(8,128)}), f32[1,4096,128]{2,1,0:T(8,128)}) %all-reduce.2.cloned.1.call-update) | async-done | bytes 2097168 | tf_op jit(solution)/shard_map/psum | solution.py:65
  506.3 5.2 fusion.23
  512.0 1.2 fusion.31
  513.3 65.9 %reduce-scatter.2.cloned.1.call-done = f32[64,256]{1,0:T(8,128)} async-done(((f32[512,256]{1,0:T(8,128)}), f32[64,256]{1,0:T(8,128)}) %reduce-scatter.2.cloned.1.call-update) | async-done | bytes 65552 | tf_op jit(solution)/shard_map/reduce_scatter | solution.py:83
  579.2 1.5 convert_element_type.21
  (56 shorter events, 3.0 us)
Async XLA Ops:
  6.5 505.5 %copy-start = (bf16[1024,256]{1,0:T(8,128)(2,1)S(1)}, bf16[1024,256]{1,0:T(8,128)(2,1)}, u32[]{:S(2)}) copy-start(bf16[1024,256]{1,0:T(8,128)(2,1)} %param.15) | copy-start | bytes 1572868
  6.5 0.8 copy-start.1
  6.5 79.2 %all-gather.2.cloned.1.call-start = ((), (), s32[]{:S(2)}) async-start(), calls=%async_computation.1 | async-start | bytes 1081344 | tf_op jit(solution)/shard_map/all_gather | solution.py:26
  7.3 499.0 %all-reduce.2.cloned.1.call-start = ((), (), s32[]{:S(2)}) async-start(), calls=%async_computation.2 | async-start | bytes 4194304 | tf_op jit(solution)/shard_map/psum | solution.py:65
  7.4 25.9 %copy-start.3 = (bf16[16,128]{1,0:T(8,128)(2,1)S(1)}, bf16[16,128]{1,0:T(8,128)(2,1)}, u32[]{:S(2)}) copy-start(bf16[16,128]{1,0:T(8,128)(2,1)} %param.12) | copy-start | bytes 12292
  93.9 5.8 copy-start.2
  108.8 5.8 copy-start.2
  123.7 5.8 copy-start.2
  138.6 5.8 copy-start.2
  153.5 5.8 copy-start.2
  168.5 5.8 copy-start.2
  183.4 5.8 copy-start.2
  198.3 5.8 copy-start.2
  322.0 7.8 %copy-start.4 = (bf16[16,128]{1,0:T(8,128)(2,1)S(1)}, bf16[16,128]{1,0:T(8,128)(2,1)}, u32[]{:S(2)}) copy-start(bf16[16,128]{1,0:T(8,128)(2,1)} %param.13) | copy-start | bytes 12292
  329.7 249.5 %reduce-scatter.2.cloned.1.call-start = ((), (), s32[]{:S(2)}) async-start(), calls=%async_computation.3 | async-start | bytes 589824 | tf_op jit(solution)/shard_map/reduce_scatter | solution.py:83
Sparse Core Ops, SparseCore 0:
  10.0 75.7 all-gather.1
  329.8 176.4 all-reduce.1
  513.4 65.7 reduce-scatter.1
where the time goes:
time: 589 us; the launch traced here: 587 us
  blocking collectives  294 us (50%)
  waiting for transfers between devices  109 us (19%)
  matrix products  85.1 us (14%)
  other arithmetic  48.1 us (8%)
  local copies, waits for them, and re-layouts  37 us (6%)
  between operations  13.2 us (2%)
    psum x1, blocking collectives, on_device(): lax.psum((state[1] * factor, state[2] * factor[..., None]), 'seq')  112 us
    pmax x1, blocking collectives, on_device(): top = lax.pmax(state[0], 'seq')  112 us
    reduce_scatter x1, waiting for transfers between devices, on_device(): lax.psum_scatter(jnp.dot(attended, out_weight, preferred_element_type=jnp...  65.9 us
    dot_general x8, matrix products, prefix_step(): jnp.einsum('kmd,nkd->kmn', query_heads, key_block, preferred_element_type...  46.3 us
    reduce_sum x9, other arithmetic, update(): total = total * factor + jnp.sum(weights, axis=2)  43.9 us
    all_gather x1, blocking collectives, on_device(): lax.all_gather(resp_keys, 'seq', axis=0, tiled=True)  38.9 us
    dot_general x9, matrix products, update(): jnp.einsum('kmn,nkd->kmd', weights.astype(jnp.bfloat16), value_block, pre...  31.9 us
    all_gather x1, blocking collectives, on_device(): lax.all_gather(resp_values, 'seq', axis=0, tiled=True)  30.9 us
  transfers between devices with their start and end apart: 3, of which 3 were waited for; matrix products, arithmetic and copies ran while one was open for 5% of the time, Pallas kernels for 0%

commit v1 on v0

v1 whole, which is shorter than its diff:
```python
import jax
import jax.numpy as jnp
from jax import lax
from jax.experimental import pallas as pl
from jax.experimental.pallas import tpu as pltpu
from jax.sharding import PartitionSpec as P

HD = 128
SCALE2 = HD**-0.5 * 1.4426950408889634
LIMIT = 64.0
SMALL = 2.0**-20
f32 = jnp.float32
bf16 = jnp.bfloat16


def attend_kernel(
    group, key_block, q_ref, k_ref, v_ref, rk_ref, rv_ref, bias_ref, out_ref,
    kt_ref, ve_ref, s_ref, logs_ref, facts_ref,
):
    head = pl.program_id(0)
    keys = k_ref.shape[0]
    rows = q_ref.shape[0]
    owners = out_ref.shape[0]
    own = rk_ref.shape[0]

    @pl.when(head == 0)
    def _():
        kt = k_ref[...].T
        kt_ref[:, :keys] = kt
        kt_ref[:, keys:] = jnp.zeros((HD, HD), bf16)
        kt_ref[:, keys : keys + HD] = jnp.concatenate(
            [rk_ref[...], jnp.zeros((HD - own, HD), bf16)], axis=0
        ).T
        ve_ref[:keys, :HD] = v_ref[...]
        ve_ref[keys:, :HD] = jnp.concatenate(
            [rv_ref[...], jnp.zeros((HD - own, HD), bf16)], axis=0
        )
        ve_ref[:, HD:] = jnp.ones((keys + HD, HD), bf16)
        logs_ref[...] = jnp.zeros_like(logs_ref)
        square = kt.astype(f32)
        facts_ref[0] = jnp.max(jnp.sum(square * square, axis=0, keepdims=True))
        facts_ref[1] = jnp.max(jnp.abs(v_ref[...].astype(f32)))

    @pl.when(head < group)
    def _():
        q = q_ref[...]

        def scores(start, size):
            return jnp.dot(q, kt_ref[:, start : start + size], preferred_element_type=f32)

        def own_scores():
            return scores(keys, HD) * SCALE2 + bias_ref[...]

        def product(weights, start, size):
            return jnp.dot(
                weights.astype(bf16), ve_ref[start : start + size, :], preferred_element_type=f32
            )

        def finish(total, shift):
            denominator = total[:, HD:]
            result = total[:, :HD] / denominator
            out_ref[...] = result.astype(bf16).reshape(owners, rows // owners, HD)
            log = jnp.log2(denominator) + shift
            high = log.astype(bf16).astype(f32)
            rest = log - high
            middle = rest.astype(bf16).astype(f32)
            low = (rest - middle).astype(bf16).astype(f32)
            lane = lax.broadcasted_iota(jnp.int32, (rows, HD), 1)
            logs_ref[...] += jnp.where(
                lane == head,
                high,
                jnp.where(
                    lane == head + group, middle, jnp.where(lane == head + 2 * group, low, 0.0)
                ),
            )

        qf = q.astype(f32)
        longest = jnp.max(jnp.sum(qf * qf, axis=1, keepdims=True))
        inside = (
            (longest * facts_ref[0] * (SCALE2 * SCALE2) <= LIMIT * LIMIT)
            & (jnp.max(own_scores()) <= LIMIT)
            & (facts_ref[1] >= SMALL)
        )

        @pl.when(inside)
        def _():
            total = product(jnp.exp2(own_scores()), keys, HD)
            now = scores(0, key_block)
            for start in range(0, keys, key_block):
                later = start + key_block
                if later < keys:
                    following = scores(later, key_block)
                total += product(jnp.exp2(now * SCALE2), start, key_block)
                if later < keys:
                    now = following
            finish(total, 0.0)

        @pl.when(jnp.logical_not(inside))
        def _():
            mine = own_scores()
            top = mine
            for start in range(0, keys, key_block):
                part = scores(start, key_block) * SCALE2
                s_ref[:, start : start + key_block] = part
                for lanes in range(0, key_block, HD):
                    top = jnp.maximum(top, part[:, lanes : lanes + HD])
            top = jnp.max(top, axis=1, keepdims=True)
            total = product(jnp.exp2(mine - top), keys, HD)
            for start in range(0, keys, key_block):
                part = s_ref[:, start : start + key_block]
                total += product(jnp.exp2(part - top), start, key_block)
            finish(total, top)

    @pl.when(head == group)
    def _():
        out_ref[...] = logs_ref[...].astype(bf16).reshape(owners, rows // owners, HD)


def attend(queries, keys, values, own_keys, own_values, bias, owners):
    rows, width = queries.shape
    group = width // HD
    count = keys.shape[0]
    tokens = rows // owners
    whole = lambda array: pl.BlockSpec(array.shape, lambda head: (0, 0))
    return pl.pallas_call(
        lambda *refs: attend_kernel(group, 256, *refs),
        grid=(group + 1,),
        out_shape=jax.ShapeDtypeStruct((owners, (group + 1) * tokens, HD), bf16),
        in_specs=[
            pl.BlockSpec((rows, HD), lambda head: (0, jnp.minimum(head, group - 1))),
            whole(keys),
            whole(values),
            whole(own_keys),
            whole(own_values),
            whole(bias),
        ],
        out_specs=pl.BlockSpec((owners, tokens, HD), lambda head: (0, head, 0)),
        scratch_shapes=[
            pltpu.VMEM((HD, count + HD), bf16),
            pltpu.VMEM((count + HD, 2 * HD), bf16),
            pltpu.VMEM((rows, count), f32),
            pltpu.VMEM((rows, HD), f32),
            pltpu.SMEM((2,), f32),
        ],
        compiler_params=pltpu.CompilerParams(vmem_limit_bytes=48 << 20),
        name="attend",
    )(queries, keys, values, own_keys, own_values, bias)


def combine_kernel(group, parts_ref, out_ref):
    owners, _, _ = parts_ref.shape
    copies, tokens, _ = out_ref.shape
    pieces = parts_ref[:, group * tokens :, :].astype(f32)
    logs = sum(pieces[:, :, piece * group : (piece + 1) * group] for piece in range(3))
    share = jnp.exp2(logs - jnp.max(logs, axis=0, keepdims=True))
    share = share / jnp.sum(share, axis=0, keepdims=True)
    for head in range(group):
        part = parts_ref[:, head * tokens : (head + 1) * tokens, :].astype(f32)
        result = jnp.sum(part * share[:, :, head : head + 1], axis=0).astype(bf16)
        out_ref[:, :, head * HD : (head + 1) * HD] = jnp.broadcast_to(
            result[None], (copies, tokens, HD)
        )


def combine(parts, copies):
    owners, height, _ = parts.shape
    tokens = 16 * (height // 144)
    group = height // tokens - 1
    return pl.pallas_call(
        lambda *refs: combine_kernel(group, *refs),
        out_shape=jax.ShapeDtypeStruct((copies, tokens, group * HD), bf16),
        compiler_params=pltpu.CompilerParams(vmem_limit_bytes=32 << 20),
        name="combine",
    )(parts)


def on_device(queries, prefix_keys, prefix_values, resp_keys, resp_values, segment_ids, out_weight):
    shards = lax.axis_size("seq")
    ways = lax.axis_size("mp")
    tokens = queries.shape[0]
    rows = segment_ids.shape[0]
    first = lax.axis_index("seq") * tokens
    own_segments = jnp.pad(lax.dynamic_slice_in_dim(segment_ids, first, tokens), (0, HD - tokens))
    column = jnp.arange(HD, dtype=jnp.int32)[None, :]
    allowed = (
        (column < tokens)
        & (segment_ids[:, None] == own_segments[None, :])
        & (first + column <= jnp.arange(rows, dtype=jnp.int32)[:, None])
    )
    bias = jnp.where(allowed, f32(0), f32(-1e30))

    copies = jnp.broadcast_to(queries[None], (shards,) + queries.shape)
    all_queries = lax.all_to_all(copies, "seq", 0, 0, tiled=True).reshape(rows, -1)
    parts = attend(
        all_queries, prefix_keys, prefix_values, resp_keys, resp_values, bias, shards
    )
    parts = lax.all_to_all(parts, "seq", 0, 0, tiled=True)
    heads = combine(parts, shards)
    heads = lax.all_to_all(heads, "seq", 0, 0, tiled=True).reshape(rows, -1)
    scored = jnp.dot(heads, out_weight, preferred_element_type=f32).astype(bf16)
    scored = scored.reshape(ways, rows // ways, -1)
    scored = lax.all_to_all(scored, "mp", 0, 0, tiled=True)
    return jnp.sum(scored.astype(f32), axis=0).astype(bf16)


def solution(mesh):
    in_specs = (
        P("seq", "mp"),
        P("seq", "mp"),
        P("seq", "mp"),
        P("seq", "mp"),
        P("seq", "mp"),
        P(),
        P("mp", "seq"),
    )
    return jax.shard_map(
        on_device, mesh=mesh, in_specs=in_specs, out_specs=P("mp", "seq"), check_vma=False
    )
```

time: 589 us -> 170 us (0.29)
  blocking collectives: 294 us -> 84.9 us
  matrix products: 85.1 us -> 0.44 us
  waiting for transfers between devices: 109 us -> 24.4 us
  other arithmetic: 48.1 us -> 0.8 us
  Pallas kernels: 0 us -> 43.2 us
  local copies, waits for them, and re-layouts: 37 us -> 3.24 us
  between operations: 13.2 us -> 0.07 us
  starting transfers between devices: 0.08 us -> 12.2 us
    psum x1 -> x0, blocking collectives: 112 us -> none  [on_device(): lax.psum((state[1] * factor, state[2] * factor[..., None]), 'seq')]
    pmax x1 -> x0, blocking collectives: 112 us -> none  [on_device(): top = lax.pmax(state[0], 'seq')]
    all_to_all x0 -> x3, blocking collectives: none -> 84.9 us  [the longest x1 37.5 us: on_device(): parts = lax.all_to_all(parts, 'seq', 0, 0, tiled=True)]
    dot_general x19 -> x1, matrix products: 85.1 us -> 0.44 us  [on_device(): scored = jnp.dot(heads, out_weight, preferred_element_type=f32).astype(bf16)]
    all_gather x2 -> x0, blocking collectives: 69.8 us -> none  [the longest x1 38.9 us: on_device(): lax.all_gather(resp_keys, 'seq', axis=0, tiled=True)]
    reduce_scatter x1 -> x0, waiting for transfers between devices: 65.9 us -> none  [on_device(): lax.psum_scatter(jnp.dot(attended, out_weight, preferred_element_type=jnp...]
    reduce_sum x9 -> x1, other arithmetic: 43.9 us -> 0.65 us  [on_device(): return jnp.sum(scored.astype(f32), axis=0).astype(bf16)]
    pallas_call x0 -> x2, Pallas kernels: none -> 43.2 us  [the longest x1 42.3 us: attend(): pl.pallas_call(lambda *refs: attend_kernel(group, 256, *refs), grid=(grou...]
  transfers between devices with their start and end apart: 3 -> 1, of which waited for: 3 -> 1; matrix products, arithmetic and copies ran while one was open for 5% -> 0% of each run, Pallas kernels for 0% -> 0%
where the time goes in v1:
time: 170 us; the launch traced here: 169 us
  blocking collectives  84.9 us (50%)
  Pallas kernels  43.2 us (25%)
  waiting for transfers between devices  24.4 us (14%)
  starting transfers between devices  12.2 us (7%)
  local copies, waits for them, and re-layouts  3.24 us (2%)
    pallas_call x1, Pallas kernels, attend(): pl.pallas_call(lambda *refs: attend_kernel(group, 256, *refs), grid=(grou...  42.3 us
    all_to_all x1, blocking collectives, on_device(): parts = lax.all_to_all(parts, 'seq', 0, 0, tiled=True)  37.5 us
    all_to_all x1, blocking collectives, on_device(): heads = lax.all_to_all(heads, 'seq', 0, 0, tiled=True).reshape(rows, -1)  31.7 us
    all_to_all x1, waiting for transfers between devices, on_device(): lax.all_to_all(copies, 'seq', 0, 0, tiled=True).reshape(rows, -1)  24.4 us
    all_to_all x1, blocking collectives, on_device(): scored = lax.all_to_all(scored, 'mp', 0, 0, tiled=True)  15.7 us
    all_to_all x1, starting transfers between devices, on_device(): lax.all_to_all(copies, 'seq', 0, 0, tiled=True).reshape(rows, -1)  12.2 us
  transfers between devices with their start and end apart: 1, of which 1 were waited for; matrix products, arithmetic and copies ran while one was open for 0% of the time, Pallas kernels for 0%

profile of v1, /device:TPU:1, one launch (start us, length us, event | category | flops | bytes accessed | tf_op | source)
XLA Modules:
  0.0 169.2 jit_solution(4087006371232875784)
XLA Ops:
  0.0 0.0 copy-start
  0.0 1.9 %broadcast_in_dim.10 = bf16[32,16,1024]{2,1,0:T(8,128)(2,1)} broadcast(bf16[16,1024]{1,0:T(8,128)(2,1)} %param.7), dimensions={1,2} | broadcast | bytes 1081344 | tf_op jit(solution)/shard_map/broadcast_in_dim | solution.py:192
  1.9 0.0 copy-start.5
  1.9 0.0 copy-start.1
  1.9 0.0 copy-start.3
  1.9 0.0 copy-start.4
  1.9 12.2 %all-to-all-start = ((bf16[32,16,1024]{2,1,0:T(8,128)(2,1)}), bf16[32,16,1024]{2,1,0:T(8,128)(2,1)S(1)}, u32[]{:S(2)}, u32[]{:S(2)}) async-start(bf16[32,16,1024]{2,1,0:T(8,128)(2,1)} %broadcast_in_dim.10), calls=%async_computation | async-start | bytes 2097152 | tf_op jit(solution)/shard_map/all_to_all | solution.py:193
  14.1 0.0 copy-done.5
  14.1 0.1 dynamic_slice.3
  14.2 0.1 fusion.1.refs_5_
  14.4 24.4 %all-to-all-done = bf16[32,16,1024]{2,1,0:T(8,128)(2,1)S(1)} async-done(((bf16[32,16,1024]{2,1,0:T(8,128)(2,1)}), bf16[32,16,1024]{2,1,0:T(8,128)(2,1)S(1)}, u32[]{:S(2)}, u32[]{:S(2)}) %all-to-all-start) | async-done | bytes 1048608 | tf_op jit(solution)/shard_map/all_to_all | solution.py:193
  38.7 0.0 copy-done.1
  38.7 0.0 copy-done.3
  38.7 0.0 copy-done.4
  38.8 0.0 copy-start.2
  38.8 1.2 copy-done.2
  40.0 42.3 %attend.1 = bf16[32,144,128]{2,1,0:T(8,128)(2,1)S(1)} custom-call(bf16[512,1024]{1,0:T(8,128)(2,1)S(1)} %bitcast.5, bf16[4096,128]{1,0:T(8,128)(2,1)S(1)} %copy-done.1, bf16[4096,128]{1,0:T(8,128)(2,1)S(1)} %copy-done.2, bf16[16,128]{1,0:T(8,128)(2,1)S(1)} %copy-done.3, bf16[16,128]{1,0:T(8,128)(2,1)S(1)} %copy-done.4, f32[512,128]{1,0:T(8,128)S(1)} %fusion.1.refs_5_), custom_call_target="tpu_custom_call" | custom-call | tf_op jit(solution)/shard_map/attend/pallas_call | solution.py:125
  82.3 37.5 %all_to_all.20.refs_0_ = bf16[32,144,128]{2,1,0:T(8,128)(2,1)S(1)} all-to-all(bf16[32,144,128]{2,1,0:T(8,128)(2,1)S(1)} %attend.1), channel_id=1, replica_groups=mesh['seq'=32,'mp'=8] {'seq'}, dimensions={0} | all-to-all | bytes 2359296 | tf_op jit(solution)/shard_map/all_to_all | solution.py:197
  119.8 0.9 combine.1
  120.8 31.7 %all_to_all.21 = bf16[32,16,1024]{2,1,0:T(8,128)(2,1)S(1)} all-to-all(bf16[32,16,1024]{2,1,0:T(8,128)(2,1)S(1)} %combine.1), channel_id=1, replica_groups=mesh['seq'=32,'mp'=8] {'seq'}, dimensions={0} | all-to-all | bytes 2097152 | tf_op jit(solution)/shard_map/all_to_all | solution.py:199
  152.4 0.0 copy-done
  152.4 0.4 convolution_convert_fusion
  152.9 15.7 %all_to_all.22 = bf16[8,64,256]{2,1,0:T(8,128)(2,1)S(1)} all-to-all(bf16[8,64,256]{2,1,0:T(8,128)(2,1)S(1)} %bitcast.7), channel_id=1, replica_groups=mesh['seq'=32,'mp'=8] {'mp'}, dimensions={0} | all-to-all | bytes 524288 | tf_op jit(solution)/shard_map/all_to_all | solution.py:202
  168.5 0.7 reduce_sum.12
  (3 shorter events, 0.0 us)
Async XLA Ops:
  0.0 152.4 %copy-start = (bf16[1024,256]{1,0:T(8,128)(2,1)S(1)}, bf16[1024,256]{1,0:T(8,128)(2,1)}, u32[]{:S(2)}) copy-start(bf16[1024,256]{1,0:T(8,128)(2,1)} %param.13) | copy-start | bytes 1572868
  1.9 12.2 %copy-start.5 = (s32[512]{0:T(512)S(1)}, s32[512]{0:T(512)}, u32[]{:S(2)}) copy-start(s32[512]{0:T(512)} %param.12) | copy-start | bytes 6148
  1.9 36.8 %copy-start.1 = (bf16[4096,128]{1,0:T(8,128)(2,1)S(1)}, bf16[4096,128]{1,0:T(8,128)(2,1)}, u32[]{:S(2)}) copy-start(bf16[4096,128]{1,0:T(8,128)(2,1)} %refs_1_.1) | copy-start | bytes 3145732
  1.9 36.8 %copy-start.3 = (bf16[16,128]{1,0:T(8,128)(2,1)S(1)}, bf16[16,128]{1,0:T(8,128)(2,1)}, u32[]{:S(2)}) copy-start(bf16[16,128]{1,0:T(8,128)(2,1)} %refs_3_.1) | copy-start | bytes 12292
  1.9 36.8 %copy-start.4 = (bf16[16,128]{1,0:T(8,128)(2,1)S(1)}, bf16[16,128]{1,0:T(8,128)(2,1)}, u32[]{:S(2)}) copy-start(bf16[16,128]{1,0:T(8,128)(2,1)} %refs_4_.1) | copy-start | bytes 12292
  1.9 36.8 %all-to-all-start = ((bf16[32,16,1024]{2,1,0:T(8,128)(2,1)}), bf16[32,16,1024]{2,1,0:T(8,128)(2,1)S(1)}, u32[]{:S(2)}, u32[]{:S(2)}) async-start(bf16[32,16,1024]{2,1,0:T(8,128)(2,1)} %broadcast_in_dim.10), calls=%async_computation | async-start | bytes 2097152 | tf_op jit(solution)/shard_map/all_to_all | solution.py:193
  38.8 1.2 copy-start.2
